TPU v7x, 32 devices: a whole 2x2x4 slice. The times are simulated.
32 devices in a mesh: lon: 4 (over y, x), lat: 8 (over z, core).
Axes of the slice: x: 2, y: 2, z: 4, core: 2. Of those that a mesh axis runs over, the one named last changes fastest.
Arguments:
- field: float32 [32, 768, 3072], P(None, 'lat', 'lon'), may hold values from -6 to 6
- vertical: float32 [32, 32], replicated, may hold values from -1.5 to 1.5, as said below
- rate: float32 [32, 768], P(None, 'lat'), may hold values from 3.2552085e-05 to 0.5
- lat_kernel: float32 [768, 768], replicated, may hold values from 0 to 1, as said below
Outputs:
- increment: float32 [32, 768, 3072], P(None, 'lat', 'lon')
Inputs may be any that keep to these rules, and one draw needn't show every extreme that they name: `vertical`: the identity plus independent terms of magnitude at most 0.5 times 4 / sqrt(32). `lat_kernel`: Non-negative weights.
All inputs are finite; a program needn't handle non-finite values.
Results may differ from a plain program's by a relative error of at most 0.00015.
Values sent between devices are 32-bit elements; how exact they have to be, the bound alone decides.
A program may use at most 128 MiB of HBM per device.

v0:
```python
import functools

import jax
import jax.numpy as jnp
from jax import lax
from jax.experimental import pallas as pl
from jax.experimental.pallas import tpu as pltpu
from jax.sharding import PartitionSpec as P

MESH = pl.DeviceIdType.MESH
LANES = 128
SUB = 8


def partner(me, step, count):
    index, bit = 0, 1
    while bit < count:
        digit = lax.rem(me // bit, 2)
        if step & bit:
            digit = 1 - digit
        index = index + digit * bit
        bit *= 2
    return index


def steps_far_first(count):
    order, top = [], count
    while top > 1:
        order += list(range(top // 2, top))
        top //= 2
    return order


def split(value):
    high = value.astype(jnp.bfloat16)
    low = (value - high.astype(jnp.float32)).astype(jnp.bfloat16)
    return high, low


def dot3(a_high, a_low, b):
    high, low = split(b)
    dot = functools.partial(jnp.dot, preferred_element_type=jnp.float32)
    return dot(a_high, high) + (dot(a_high, low) + dot(a_low, high))


def kernel(
    n_lon, n_lat,
    field, mixer, packed, weights, out,
    mix_high, mix_low, w_high, w_low, rows, edges, edges_in, state, gathered, smooth,
    edge_send, edge_recv, x_send, x_recv, y_send, y_recv, own_sem,
):
    lon, lat = lax.axis_index("lon"), lax.axis_index("lat")
    rounds, levels, depth, width = rows.shape
    groups, chunks = depth // SUB, width // LANES
    order = steps_far_first(n_lat)
    lane = lax.broadcasted_iota(jnp.int32, (SUB, LANES), 1)
    ahead = (lane + 1).astype(jnp.float32)
    behind = (LANES - lane).astype(jnp.float32)

    barrier = pltpu.get_barrier_semaphore()
    for step in range(1, n_lon):
        pl.semaphore_signal(barrier, inc=1, device_id={"lon": lax.rem(lon + step, n_lon)}, device_id_type=MESH)
    for step in order:
        pl.semaphore_signal(barrier, inc=1, device_id={"lat": partner(lat, step, n_lat)}, device_id_type=MESH)

    def pick(values, index):
        one = jnp.sum(jnp.where(lane == index, values, 0.0), axis=1, keepdims=True)
        return jnp.broadcast_to(one, (SUB, LANES))

    def column(values, index):
        return jnp.broadcast_to(values[:, index : index + 1], (SUB, LANES))

    def group_rows(g):
        return pl.ds(pl.multiple_of(g * SUB, SUB), SUB)

    def edge_copy(q, step):
        return pltpu.make_async_remote_copy(
            src_ref=edges.at[q], dst_ref=edges_in.at[q, step - 1],
            send_sem=edge_send.at[q, step - 1], recv_sem=edge_recv.at[q, step - 1],
            device_id={"lon": lax.rem(lon + step, n_lon)}, device_id_type=MESH,
        )

    def x_copy(q, step):
        target = partner(lat, step, n_lat)
        return pltpu.make_async_remote_copy(
            src_ref=rows.at[q, target],
            dst_ref=gathered.at[q, pl.ds(pl.multiple_of(lat * depth, SUB), depth)],
            send_sem=x_send.at[q, step - 1], recv_sem=x_recv.at[q, step - 1],
            device_id={"lat": target}, device_id_type=MESH,
        )

    def y_copy(q, step):
        target = partner(lat, step, n_lat)
        return pltpu.make_async_remote_copy(
            src_ref=smooth.at[q, pl.ds(pl.multiple_of(target * depth, SUB), depth)],
            dst_ref=out.at[lat * rounds + q],
            send_sem=y_send.at[q, step - 1], recv_sem=y_recv.at[q, step - 1],
            device_id={"lat": target}, device_id_type=MESH,
        )

    def own_copy(q):
        return pltpu.make_async_copy(
            smooth.at[q, pl.ds(pl.multiple_of(lat * depth, SUB), depth)],
            out.at[lat * rounds + q], own_sem.at[q],
        )

    for q in range(rounds):
        mix_high[q], mix_low[q] = split(mixer[q])

    def scan_group(q, g):
        here = group_rows(g)
        x = field[:, here, :]
        x = x.reshape(x.shape[0] * SUB, width)
        mixed = dot3(mix_high[q], mix_low[q], x)
        rows[q, :, here, :] = mixed.reshape(levels, SUB, width)
        logs = packed[0, q, here, :]

        def level(t, acc):
            log = pick(logs, 2 * t)
            power = jnp.exp(log)
            east, west = [], []
            for k in range(7):
                east.append(jnp.where(lane >= 2**k, power, 0.0))
                west.append(jnp.where(lane < LANES - 2**k, power, 0.0))
                power = power * power
            stride = jnp.exp(log * float(LANES))
            to_east, to_west = jnp.exp(log * ahead), jnp.exp(log * behind)
            sums, ys, zs = [], [], []
            for c in range(chunks):
                v = rows[q, t, here, c * LANES : (c + 1) * LANES]
                y = z = v
                for k in range(7):
                    y = y + east[k] * pltpu.roll(y, 2**k, 1)
                    z = z + west[k] * pltpu.roll(z, LANES - 2**k, 1)
                ys.append(column(y, LANES - 1))
                zs.append(column(z, 0))
                sums.append(y + z - v)
            carry = ys[0]
            for c in range(1, chunks):
                sums[c] = sums[c] + to_east * carry
                carry = ys[c] + stride * carry
            back = zs[chunks - 1]
            for c in range(chunks - 2, -1, -1):
                sums[c] = sums[c] + to_west * back
                back = zs[c] + stride * back
            for c in range(chunks):
                rows[q, t, here, c * LANES : (c + 1) * LANES] = sums[c]
            return jnp.where(lane == 2 * t, carry, jnp.where(lane == 2 * t + 1, back, acc))

        edges[q, here, :] = lax.fori_loop(0, levels, level, jnp.zeros((SUB, LANES), jnp.float32))

    def state_group(q, g):
        here = group_rows(g)
        log = packed[0, q, here, :] * float(width)
        eastward = lax.rem(lane, 2) == 0
        total = edges[q, here, :] * jnp.exp(log * float(n_lon - 1))
        for step in range(1, n_lon):
            hops = jnp.where(eastward, float(step - 1), float(n_lon - step - 1))
            total = total + edges_in[q, step - 1, here, :] * jnp.exp(log * hops)
        state[here, :] = total / (1.0 - jnp.exp(log * float(n_lon)))

    def correct(q, step):
        t = partner(lat, step, n_lat)

        def group(g, _):
            here = group_rows(g)
            log = pick(packed[0, q, here, :], 2 * t)
            scale = pick(packed[1, q, here, :], 2 * t)
            incoming = state[here, :]
            carry = pick(incoming, 2 * t) * scale
            back = pick(incoming, 2 * t + 1) * scale
            stride = jnp.exp(log * float(LANES))
            to_east, to_west = jnp.exp(log * ahead), jnp.exp(log * behind)
            parts = []
            for c in range(chunks):
                parts.append(scale * rows[q, t, here, c * LANES : (c + 1) * LANES] + to_east * carry)
                carry = carry * stride
            for c in range(chunks - 1, -1, -1):
                parts[c] = parts[c] + to_west * back
                back = back * stride
            for c in range(chunks):
                at = slice(c * LANES, (c + 1) * LANES)
                if step == 0:
                    gathered[q, pl.ds(pl.multiple_of(lat * depth + g * SUB, SUB), SUB), at] = parts[c]
                else:
                    rows[q, t, here, at] = parts[c]
            return 0

        lax.fori_loop(0, groups, group, 0)

    def first(q, _):
        def scan(g, _):
            scan_group(q, g)
            return 0

        lax.fori_loop(0, groups, scan, 0)

        @pl.when(q == 0)
        def _():
            pl.semaphore_wait(barrier, n_lon - 1 + n_lat - 1)

        for step in range(1, n_lon):
            edge_copy(q, step).start()
        for step in range(1, n_lon):
            edge_copy(q, step).wait()

        def states(g, _):
            state_group(q, g)
            return 0

        lax.fori_loop(0, groups, states, 0)
        for step in order:
            correct(q, step)
            x_copy(q, step).start()
        correct(q, 0)
        return 0

    lax.fori_loop(0, rounds, first, 0)
    w_high[...], w_low[...] = split(weights[...])

    def second(q, _):
        for step in order:
            x_copy(q, step).wait_recv()
        tile = 256 if width % 256 == 0 else LANES

        def columns(n, _):
            at = pl.ds(pl.multiple_of(n * tile, tile), tile)
            smooth[q, :, at] = dot3(w_high[...], w_low[...], gathered[q, :, at])
            return 0

        lax.fori_loop(0, width // tile, columns, 0)
        for step in order:
            y_copy(q, step).start()
        own_copy(q).start()
        return 0

    lax.fori_loop(0, rounds, second, 0)

    def finish(q, _):
        own_copy(q).wait()
        for step in order:
            x_copy(q, step).wait_send()
            y_copy(q, step).wait()
        return 0

    lax.fori_loop(0, rounds, finish, 0)


def on_device(n_lon, n_lat, field, vertical, rate, lat_kernel):
    lev, depth, width = field.shape
    total = depth * n_lat
    rounds = lev // n_lat
    f32, bf16 = jnp.float32, jnp.bfloat16
    by_round = vertical.reshape(n_lat, rounds, lev).transpose(1, 0, 2)
    mixer = (by_round[:, :, None, :, None] * jnp.eye(SUB, dtype=f32)[None, None, :, None, :]).reshape(
        rounds, n_lat * SUB, lev * SUB
    )
    pair = jnp.stack([jnp.log1p(-rate), rate / (2.0 - rate)])
    pair = pair.reshape(2, n_lat, rounds, depth).transpose(0, 2, 3, 1)
    packed = jnp.pad(jnp.repeat(pair, 2, axis=3), ((0, 0), (0, 0), (0, 0), (0, LANES - 2 * n_lat)), constant_values=-1.0)
    vmem, dma = pltpu.VMEM, pltpu.SemaphoreType.DMA
    return pl.pallas_call(
        functools.partial(kernel, n_lon, n_lat),
        out_shape=jax.ShapeDtypeStruct(field.shape, f32),
        in_specs=[pl.BlockSpec(memory_space=pltpu.VMEM)] * 4,
        out_specs=pl.BlockSpec(memory_space=pl.ANY),
        scratch_shapes=[
            vmem((rounds, n_lat * SUB, lev * SUB), bf16),
            vmem((rounds, n_lat * SUB, lev * SUB), bf16),
            vmem((total, total), bf16),
            vmem((total, total), bf16),
            vmem((rounds, n_lat, depth, width), f32),
            vmem((rounds, depth, LANES), f32),
            vmem((rounds, n_lon - 1, depth, LANES), f32),
            vmem((depth, LANES), f32),
            vmem((rounds, total, width), f32),
            vmem((rounds, total, width), f32),
            dma((rounds, n_lon - 1)),
            dma((rounds, n_lon - 1)),
            dma((rounds, n_lat - 1)),
            dma((rounds, n_lat - 1)),
            dma((rounds, n_lat - 1)),
            dma((rounds, n_lat - 1)),
            dma((rounds,)),
        ],
        compiler_params=pltpu.CompilerParams(
            collective_id=0, has_side_effects=True, vmem_limit_bytes=60 * 1024 * 1024
        ),
        cost_estimate=pl.CostEstimate(
            flops=6 * lev * depth * width * (total + lev), bytes_accessed=8 * lev * depth * width, transcendentals=0
        ),
    )(field, mixer, packed, lat_kernel)


def solution(mesh):
    return jax.shard_map(
        functools.partial(on_device, mesh.shape["lon"], mesh.shape["lat"]),
        mesh=mesh,
        in_specs=(P(None, "lat", "lon"), P(), P(None, "lat"), P()),
        out_specs=P(None, "lat", "lon"),
        check_vma=False,
    )
```

profile of v0, /device:TPU:9, one launch (start us, length us, event | category | flops | bytes accessed | tf_op | source)
XLA Modules:
  0.0 566.6 jit_solution(14434328105459915479)
XLA Ops:
  0.0 0.7 copy.7
  0.7 0.7 negate_log-plus-one_fusion
  1.5 0.2 copy.9
  1.7 0.8 pad.4.packed
  2.5 0.1 mul.22
  2.6 0.5 mul.23
  3.1 2.6 mul.20
  5.7 4.0 mul.21
  9.7 0.7 broadcast_multiply_fusion.mixer
  10.5 547.7 %shard_map.46 = f32[32,96,768]{2,1,0:T(8,128)} custom-call(f32[32,96,768]{2,1,0:T(8,128)} %field.1, f32[4,64,256]{2,1,0:T(8,128)} %broadcast_multiply_fusion.mixer, f32[2,4,96,128]{3,2,1,0:T(8,128)} %pad.4.packed, f32[768,768]{1,0:T(8,128)} %weights.1), custom_call_target="tpu_custom_call" | custom-call | flops 11324620800 | bytes 18874368 | tf_op jit(solution)/shard_map/pallas_call | solution.py:262
  558.1 8.4 %copy.11 = f32[32,96,768]{2,1,0:T(8,128)} copy(f32[32,96,768]{2,1,0:T(8,128)} %shard_map.46) | data formatting | bytes 18874368
  (4 shorter events, 0.0 us)
where the time goes:
time: 567 us
  Pallas kernels  548 us (97%)
  local copies, waits for them, and re-layouts  17.4 us (3%)
    pallas_call x1, Pallas kernels, on_device(): pl.pallas_call(functools.partial(kernel, n_lon, n_lat), out_shape=jax.Sha...  548 us

commit v1 on v0

--- a/solution.py
+++ b/solution.py
@@ -15,20 +15,14 @@
 def partner(me, step, count):
     index, bit = 0, 1
     while bit < count:
-        digit = lax.rem(me // bit, 2)
-        if step & bit:
-            digit = 1 - digit
-        index = index + digit * bit
+        index = index + lax.rem(me // bit + step // bit, 2) * bit
         bit *= 2
     return index
 
 
-def steps_far_first(count):
-    order, top = [], count
-    while top > 1:
-        order += list(range(top // 2, top))
-        top //= 2
-    return order
+def step_at(me, place, count):
+    turn = lax.rem(me, count // 2)
+    return lax.rem(place - turn + count - 1, count - 1) + 1
 
 
 def split(value):
@@ -45,14 +39,14 @@
 
 def kernel(
     n_lon, n_lat,
-    field, mixer, packed, weights, out,
-    mix_high, mix_low, w_high, w_low, rows, edges, edges_in, state, gathered, smooth,
-    edge_send, edge_recv, x_send, x_recv, y_send, y_recv, own_sem,
+    field_hbm, vertical, packed, weights_hbm, out,
+    field, weights, mix_high, mix_low, w_high, w_low, rows, edges, edges_in, state, gathered, smooth,
+    edge_send, edge_recv, x_send, x_recv, y_send, y_recv, own_sem, field_sem, weights_sem,
 ):
     lon, lat = lax.axis_index("lon"), lax.axis_index("lat")
     rounds, levels, depth, width = rows.shape
     groups, chunks = depth // SUB, width // LANES
-    order = steps_far_first(n_lat)
+    order = range(1, n_lat)
     lane = lax.broadcasted_iota(jnp.int32, (SUB, LANES), 1)
     ahead = (lane + 1).astype(jnp.float32)
     behind = (LANES - lane).astype(jnp.float32)
@@ -104,8 +98,31 @@
             out.at[lat * rounds + q], own_sem.at[q],
         )
 
+    def field_copy(g):
+        return pltpu.make_async_copy(
+            field_hbm.at[:, group_rows(g), :], field.at[:, group_rows(g), :], field_sem.at[g]
+        )
+
+    def load(g, _):
+        field_copy(g).start()
+        return 0
+
+    weights_copy = pltpu.make_async_copy(weights_hbm, weights, weights_sem)
+    lax.fori_loop(0, groups, load, 0)
+    weights_copy.start()
+
+    wide, lev = levels * SUB, vertical.shape[0]
+    one_hot = lambda hit: jnp.where(hit, 1.0, 0.0).astype(jnp.bfloat16)
+    dot = functools.partial(jnp.dot, preferred_element_type=jnp.float32)
+    iota = lambda shape, axis: lax.broadcasted_iota(jnp.int32, shape, axis)
+    spread = one_hot(iota((lev, lev * SUB), 0) == lax.shift_right_logical(iota((lev, lev * SUB), 1), 3))
+    grid = (wide, lev * SUB)
+    same = lax.bitwise_and(iota(grid, 0), SUB - 1) == lax.bitwise_and(iota(grid, 1), SUB - 1)
     for q in range(rounds):
-        mix_high[q], mix_low[q] = split(mixer[q])
+        chosen = one_hot(lax.shift_right_logical(iota((wide, lev), 0), 3) * rounds + q == iota((wide, lev), 1))
+        for half, target in zip(split(vertical[...]), (mix_high, mix_low)):
+            picked = dot(chosen, half).astype(jnp.bfloat16)
+            target[q] = jnp.where(same, dot(picked, spread), 0.0).astype(jnp.bfloat16)
 
     def scan_group(q, g):
         here = group_rows(g)
@@ -159,9 +176,13 @@
             total = total + edges_in[q, step - 1, here, :] * jnp.exp(log * hops)
         state[here, :] = total / (1.0 - jnp.exp(log * float(n_lon)))
 
-    def correct(q, step):
-        t = partner(lat, step, n_lat)
-
+    def set_row(q, t, g, at, part):
+        rows[q, t, group_rows(g), at] = part
+
+    def set_own(q, g, at, part):
+        gathered[q, pl.ds(pl.multiple_of(lat * depth + g * SUB, SUB), SUB), at] = part
+
+    def correct(q, t, store):
         def group(g, _):
             here = group_rows(g)
             log = pick(packed[0, q, here, :], 2 * t)
@@ -180,16 +201,17 @@
                 back = back * stride
             for c in range(chunks):
                 at = slice(c * LANES, (c + 1) * LANES)
-                if step == 0:
-                    gathered[q, pl.ds(pl.multiple_of(lat * depth + g * SUB, SUB), SUB), at] = parts[c]
-                else:
-                    rows[q, t, here, at] = parts[c]
+                store(g, at, parts[c])
             return 0
 
         lax.fori_loop(0, groups, group, 0)
 
     def first(q, _):
         def scan(g, _):
+            @pl.when(q == 0)
+            def _():
+                field_copy(g).wait()
+
             scan_group(q, g)
             return 0
 
@@ -209,13 +231,20 @@
             return 0
 
         lax.fori_loop(0, groups, states, 0)
-        for step in order:
-            correct(q, step)
+
+        def ship(place, _):
+            step = step_at(lat, place, n_lat)
+            t = partner(lat, step, n_lat)
+            correct(q, t, lambda g, at, part: set_row(q, t, g, at, part))
             x_copy(q, step).start()
-        correct(q, 0)
+            return 0
+
+        lax.fori_loop(0, n_lat - 1, ship, 0)
+        correct(q, lat, lambda g, at, part: set_own(q, g, at, part))
         return 0
 
     lax.fori_loop(0, rounds, first, 0)
+    weights_copy.wait()
     w_high[...], w_low[...] = split(weights[...])
 
     def second(q, _):
@@ -229,8 +258,12 @@
             return 0
 
         lax.fori_loop(0, width // tile, columns, 0)
-        for step in order:
-            y_copy(q, step).start()
+
+        def ship(place, _):
+            y_copy(q, step_at(lat, place, n_lat)).start()
+            return 0
+
+        lax.fori_loop(0, n_lat - 1, ship, 0)
         own_copy(q).start()
         return 0
 
@@ -251,10 +284,6 @@
     total = depth * n_lat
     rounds = lev // n_lat
     f32, bf16 = jnp.float32, jnp.bfloat16
-    by_round = vertical.reshape(n_lat, rounds, lev).transpose(1, 0, 2)
-    mixer = (by_round[:, :, None, :, None] * jnp.eye(SUB, dtype=f32)[None, None, :, None, :]).reshape(
-        rounds, n_lat * SUB, lev * SUB
-    )
     pair = jnp.stack([jnp.log1p(-rate), rate / (2.0 - rate)])
     pair = pair.reshape(2, n_lat, rounds, depth).transpose(0, 2, 3, 1)
     packed = jnp.pad(jnp.repeat(pair, 2, axis=3), ((0, 0), (0, 0), (0, 0), (0, LANES - 2 * n_lat)), constant_values=-1.0)
@@ -262,9 +291,16 @@
     return pl.pallas_call(
         functools.partial(kernel, n_lon, n_lat),
         out_shape=jax.ShapeDtypeStruct(field.shape, f32),
-        in_specs=[pl.BlockSpec(memory_space=pltpu.VMEM)] * 4,
+        in_specs=[
+            pl.BlockSpec(memory_space=pl.ANY),
+            pl.BlockSpec(memory_space=pltpu.VMEM),
+            pl.BlockSpec(memory_space=pltpu.VMEM),
+            pl.BlockSpec(memory_space=pl.ANY),
+        ],
         out_specs=pl.BlockSpec(memory_space=pl.ANY),
         scratch_shapes=[
+            vmem(field.shape, f32),
+            vmem((total, total), f32),
             vmem((rounds, n_lat * SUB, lev * SUB), bf16),
             vmem((rounds, n_lat * SUB, lev * SUB), bf16),
             vmem((total, total), bf16),
@@ -282,6 +318,8 @@
             dma((rounds, n_lat - 1)),
             dma((rounds, n_lat - 1)),
             dma((rounds,)),
+            dma((depth // SUB,)),
+            dma(()),
         ],
         compiler_params=pltpu.CompilerParams(
             collective_id=0, has_side_effects=True, vmem_limit_bytes=60 * 1024 * 1024
@@ -289,7 +327,7 @@
         cost_estimate=pl.CostEstimate(
             flops=6 * lev * depth * width * (total + lev), bytes_accessed=8 * lev * depth * width, transcendentals=0
         ),
-    )(field, mixer, packed, lat_kernel)
+    )(field, vertical, packed, lat_kernel)
 
 
 def solution(mesh):

time: 567 us -> 556 us (0.981)
  local copies, waits for them, and re-layouts: 17.4 us -> 9.38 us
    mul x4 -> x0, local copies, waits for them, and re-layouts: 7.26 us -> none  [on_device(): by_round[:, :, None, :, None]]
where the time goes in v1:
time: 556 us
  Pallas kernels  546 us (98%)
  local copies, waits for them, and re-layouts  9.38 us (2%)
    pallas_call x1, Pallas kernels, on_device(): pl.pallas_call(functools.partial(kernel, n_lon, n_lat), out_shape=jax.Sha...  546 us

profile of v1, /device:TPU:9, one launch (start us, length us, event | category | flops | bytes accessed | tf_op | source)
XLA Modules:
  0.0 555.7 jit_solution(11744592204011516517)
XLA Ops:
  0.0 0.7 negate_log-plus-one_fusion
  0.8 0.2 copy.7
  1.0 0.8 pad.4.packed
  1.7 545.6 %shard_map.46 = f32[32,96,768]{2,1,0:T(8,128)} custom-call(f32[32,96,768]{2,1,0:T(8,128)} %field_hbm.1, f32[32,32]{1,0:T(8,128)} %vertical.1, f32[2,4,96,128]{3,2,1,0:T(8,128)} %pad.4.packed, f32[768,768]{1,0:T(8,128)} %weights_hbm.1), custom_call_target="tpu_custom_call" | custom-call | flops 11324620800 | bytes 18874368 | tf_op jit(solution)/shard_map/pallas_call | solution.py:291
  547.3 8.4 %copy.9 = f32[32,96,768]{2,1,0:T(8,128)} copy(f32[32,96,768]{2,1,0:T(8,128)} %shard_map.46) | data formatting | bytes 18874368
  (3 shorter events, 0.0 us)

commit v2 on v1

--- a/solution.py
+++ b/solution.py
@@ -47,22 +47,12 @@
     rounds, levels, depth, width = rows.shape
     groups, chunks = depth // SUB, width // LANES
     order = range(1, n_lat)
-    lane = lax.broadcasted_iota(jnp.int32, (SUB, LANES), 1)
-    ahead = (lane + 1).astype(jnp.float32)
-    behind = (LANES - lane).astype(jnp.float32)
 
     barrier = pltpu.get_barrier_semaphore()
     for step in range(1, n_lon):
         pl.semaphore_signal(barrier, inc=1, device_id={"lon": lax.rem(lon + step, n_lon)}, device_id_type=MESH)
     for step in order:
         pl.semaphore_signal(barrier, inc=1, device_id={"lat": partner(lat, step, n_lat)}, device_id_type=MESH)
-
-    def pick(values, index):
-        one = jnp.sum(jnp.where(lane == index, values, 0.0), axis=1, keepdims=True)
-        return jnp.broadcast_to(one, (SUB, LANES))
-
-    def column(values, index):
-        return jnp.broadcast_to(values[:, index : index + 1], (SUB, LANES))
 
     def group_rows(g):
         return pl.ds(pl.multiple_of(g * SUB, SUB), SUB)
@@ -124,87 +114,94 @@
             picked = dot(chosen, half).astype(jnp.bfloat16)
             target[q] = jnp.where(same, dot(picked, spread), 0.0).astype(jnp.bfloat16)
 
+    def spread_lane(values, index):
+        one = jnp.sum(jnp.where(lane_of(values) == index, values, 0.0), axis=1, keepdims=True)
+        return jnp.broadcast_to(one, values.shape)
+
+    def lane_of(values):
+        return lax.broadcasted_iota(jnp.int32, values.shape, 1)
+
+    def column(values, index):
+        return jnp.broadcast_to(values[:, index : index + 1], values.shape)
+
+    def powers(log):
+        place = lane_of(log)
+        ahead = (place + 1).astype(jnp.float32)
+        behind = (LANES - place).astype(jnp.float32)
+        return jnp.exp(log * float(LANES)), jnp.exp(log * ahead), jnp.exp(log * behind)
+
     def scan_group(q, g):
         here = group_rows(g)
         x = field[:, here, :]
         x = x.reshape(x.shape[0] * SUB, width)
         mixed = dot3(mix_high[q], mix_low[q], x)
-        rows[q, :, here, :] = mixed.reshape(levels, SUB, width)
         logs = packed[0, q, here, :]
-
-        def level(t, acc):
-            log = pick(logs, 2 * t)
-            power = jnp.exp(log)
-            east, west = [], []
+        log = jnp.concatenate([spread_lane(logs, 2 * t) for t in range(levels)], axis=0)
+        stride, to_east, to_west = powers(log)
+        place = lane_of(log)
+        power = jnp.exp(log)
+        east, west = [], []
+        for k in range(7):
+            east.append(jnp.where(place >= 2**k, power, 0.0))
+            west.append(jnp.where(place < LANES - 2**k, power, 0.0))
+            power = power * power
+        sums, ys, zs = [], [], []
+        for c in range(chunks):
+            v = mixed[:, c * LANES : (c + 1) * LANES]
+            y = z = v
             for k in range(7):
-                east.append(jnp.where(lane >= 2**k, power, 0.0))
-                west.append(jnp.where(lane < LANES - 2**k, power, 0.0))
-                power = power * power
-            stride = jnp.exp(log * float(LANES))
-            to_east, to_west = jnp.exp(log * ahead), jnp.exp(log * behind)
-            sums, ys, zs = [], [], []
-            for c in range(chunks):
-                v = rows[q, t, here, c * LANES : (c + 1) * LANES]
-                y = z = v
-                for k in range(7):
-                    y = y + east[k] * pltpu.roll(y, 2**k, 1)
-                    z = z + west[k] * pltpu.roll(z, LANES - 2**k, 1)
-                ys.append(column(y, LANES - 1))
-                zs.append(column(z, 0))
-                sums.append(y + z - v)
-            carry = ys[0]
-            for c in range(1, chunks):
-                sums[c] = sums[c] + to_east * carry
-                carry = ys[c] + stride * carry
-            back = zs[chunks - 1]
-            for c in range(chunks - 2, -1, -1):
-                sums[c] = sums[c] + to_west * back
-                back = zs[c] + stride * back
-            for c in range(chunks):
-                rows[q, t, here, c * LANES : (c + 1) * LANES] = sums[c]
-            return jnp.where(lane == 2 * t, carry, jnp.where(lane == 2 * t + 1, back, acc))
-
-        edges[q, here, :] = lax.fori_loop(0, levels, level, jnp.zeros((SUB, LANES), jnp.float32))
-
-    def state_group(q, g):
-        here = group_rows(g)
-        log = packed[0, q, here, :] * float(width)
-        eastward = lax.rem(lane, 2) == 0
-        total = edges[q, here, :] * jnp.exp(log * float(n_lon - 1))
+                y = y + east[k] * pltpu.roll(y, 2**k, 1)
+                z = z + west[k] * pltpu.roll(z, LANES - 2**k, 1)
+            ys.append(column(y, LANES - 1))
+            zs.append(column(z, 0))
+            sums.append(y + z - v)
+        carry = ys[0]
+        for c in range(1, chunks):
+            sums[c] = sums[c] + to_east * carry
+            carry = ys[c] + stride * carry
+        back = zs[chunks - 1]
+        for c in range(chunks - 2, -1, -1):
+            sums[c] = sums[c] + to_west * back
+            back = zs[c] + stride * back
+        for c in range(chunks):
+            rows[q, :, here, c * LANES : (c + 1) * LANES] = sums[c].reshape(levels, SUB, LANES)
+        edge = jnp.zeros((SUB, LANES), jnp.float32)
+        lane = lane_of(edge)
+        for t in range(levels):
+            part = slice(t * SUB, (t + 1) * SUB)
+            edge = jnp.where(lane == 2 * t, carry[part], jnp.where(lane == 2 * t + 1, back[part], edge))
+        edges[q, here, :] = edge
+
+    def find_state(q):
+        log = packed[0, q] * float(width)
+        eastward = lax.rem(lane_of(log), 2) == 0
+        total = edges[q] * jnp.exp(log * float(n_lon - 1))
         for step in range(1, n_lon):
             hops = jnp.where(eastward, float(step - 1), float(n_lon - step - 1))
-            total = total + edges_in[q, step - 1, here, :] * jnp.exp(log * hops)
-        state[here, :] = total / (1.0 - jnp.exp(log * float(n_lon)))
-
-    def set_row(q, t, g, at, part):
-        rows[q, t, group_rows(g), at] = part
-
-    def set_own(q, g, at, part):
-        gathered[q, pl.ds(pl.multiple_of(lat * depth + g * SUB, SUB), SUB), at] = part
+            total = total + edges_in[q, step - 1] * jnp.exp(log * hops)
+        state[...] = total / (1.0 - jnp.exp(log * float(n_lon)))
+
+    def set_row(q, t, at, part):
+        rows[q, t, :, at] = part
+
+    def set_own(q, at, part):
+        gathered[q, pl.ds(pl.multiple_of(lat * depth, SUB), depth), at] = part
 
     def correct(q, t, store):
-        def group(g, _):
-            here = group_rows(g)
-            log = pick(packed[0, q, here, :], 2 * t)
-            scale = pick(packed[1, q, here, :], 2 * t)
-            incoming = state[here, :]
-            carry = pick(incoming, 2 * t) * scale
-            back = pick(incoming, 2 * t + 1) * scale
-            stride = jnp.exp(log * float(LANES))
-            to_east, to_west = jnp.exp(log * ahead), jnp.exp(log * behind)
-            parts = []
-            for c in range(chunks):
-                parts.append(scale * rows[q, t, here, c * LANES : (c + 1) * LANES] + to_east * carry)
-                carry = carry * stride
-            for c in range(chunks - 1, -1, -1):
-                parts[c] = parts[c] + to_west * back
-                back = back * stride
-            for c in range(chunks):
-                at = slice(c * LANES, (c + 1) * LANES)
-                store(g, at, parts[c])
-            return 0
-
-        lax.fori_loop(0, groups, group, 0)
+        incoming = state[...]
+        scale = spread_lane(packed[1, q], 2 * t)
+        stride, to_east, to_west = powers(spread_lane(packed[0, q], 2 * t))
+        carry = spread_lane(incoming, 2 * t) * scale
+        back = spread_lane(incoming, 2 * t + 1) * scale
+        parts = []
+        for c in range(chunks):
+            parts.append(scale * rows[q, t, :, c * LANES : (c + 1) * LANES] + to_east * carry)
+            carry = carry * stride
+        for c in range(chunks - 1, -1, -1):
+            parts[c] = parts[c] + to_west * back
+            back = back * stride
+        for c in range(chunks):
+            store(slice(c * LANES, (c + 1) * LANES), parts[c])
 
     def first(q, _):
         def scan(g, _):
@@ -226,21 +223,17 @@
         for step in range(1, n_lon):
             edge_copy(q, step).wait()
 
-        def states(g, _):
-            state_group(q, g)
-            return 0
-
-        lax.fori_loop(0, groups, states, 0)
+        find_state(q)
 
         def ship(place, _):
             step = step_at(lat, place, n_lat)
             t = partner(lat, step, n_lat)
-            correct(q, t, lambda g, at, part: set_row(q, t, g, at, part))
+            correct(q, t, functools.partial(set_row, q, t))
             x_copy(q, step).start()
             return 0
 
         lax.fori_loop(0, n_lat - 1, ship, 0)
-        correct(q, lat, lambda g, at, part: set_own(q, g, at, part))
+        correct(q, lat, functools.partial(set_own, q))
         return 0
 
     lax.fori_loop(0, rounds, first, 0)

time: 556 us -> 441 us (0.79)
  Pallas kernels: 546 us -> 431 us
    pallas_call x1, Pallas kernels: 546 us -> 431 us  [on_device(): pl.pallas_call(functools.partial(kernel, n_lon, n_lat), out_shape=jax.Sha...]
where the time goes in v2:
time: 441 us
  Pallas kernels  431 us (98%)
  local copies, waits for them, and re-layouts  9.38 us (2%)
    pallas_call x1, Pallas kernels, on_device(): pl.pallas_call(functools.partial(kernel, n_lon, n_lat), out_shape=jax.Sha...  431 us

profile of v2, /device:TPU:9, one launch (start us, length us, event | category | flops | bytes accessed | tf_op | source)
XLA Modules:
  0.0 440.7 jit_solution(13807075851518450783)
XLA Ops:
  0.0 0.7 negate_log-plus-one_fusion
  0.8 0.2 copy.7
  1.0 0.8 pad.4.packed
  1.7 430.5 %shard_map.46 = f32[32,96,768]{2,1,0:T(8,128)} custom-call(f32[32,96,768]{2,1,0:T(8,128)} %field_hbm.1, f32[32,32]{1,0:T(8,128)} %vertical.1, f32[2,4,96,128]{3,2,1,0:T(8,128)} %pad.4.packed, f32[768,768]{1,0:T(8,128)} %weights_hbm.1), custom_call_target="tpu_custom_call" | custom-call | flops 11324620800 | bytes 18874368 | tf_op jit(solution)/shard_map/pallas_call | solution.py:284
  432.3 8.4 %copy.9 = f32[32,96,768]{2,1,0:T(8,128)} copy(f32[32,96,768]{2,1,0:T(8,128)} %shard_map.46) | data formatting | bytes 18874368
  (3 shorter events, 0.0 us)

commit v3 on v2

--- a/solution.py
+++ b/solution.py
@@ -46,6 +46,8 @@
     lon, lat = lax.axis_index("lon"), lax.axis_index("lat")
     rounds, levels, depth, width = rows.shape
     groups, chunks = depth // SUB, width // LANES
+    parts = x_send.shape[1]
+    part = depth // parts
     order = range(1, n_lat)
 
     barrier = pltpu.get_barrier_semaphore()
@@ -57,19 +59,24 @@
     def group_rows(g):
         return pl.ds(pl.multiple_of(g * SUB, SUB), SUB)
 
-    def edge_copy(q, step):
+    def part_rows(h):
+        return pl.ds(pl.multiple_of(h * part, SUB), part)
+
+    def part_gathered(h):
+        return pl.ds(pl.multiple_of(lat * depth + h * part, SUB), part)
+
+    def edge_copy(q, h, step):
         return pltpu.make_async_remote_copy(
-            src_ref=edges.at[q], dst_ref=edges_in.at[q, step - 1],
-            send_sem=edge_send.at[q, step - 1], recv_sem=edge_recv.at[q, step - 1],
+            src_ref=edges.at[q, part_rows(h)], dst_ref=edges_in.at[q, step - 1, part_rows(h)],
+            send_sem=edge_send.at[q, h, step - 1], recv_sem=edge_recv.at[q, h, step - 1],
             device_id={"lon": lax.rem(lon + step, n_lon)}, device_id_type=MESH,
         )
 
-    def x_copy(q, step):
+    def x_copy(q, h, step):
         target = partner(lat, step, n_lat)
         return pltpu.make_async_remote_copy(
-            src_ref=rows.at[q, target],
-            dst_ref=gathered.at[q, pl.ds(pl.multiple_of(lat * depth, SUB), depth)],
-            send_sem=x_send.at[q, step - 1], recv_sem=x_recv.at[q, step - 1],
+            src_ref=rows.at[q, target, part_rows(h)], dst_ref=gathered.at[q, part_gathered(h)],
+            send_sem=x_send.at[q, h, step - 1], recv_sem=x_recv.at[q, h, step - 1],
             device_id={"lat": target}, device_id_type=MESH,
         )
 
@@ -168,43 +175,49 @@
         edge = jnp.zeros((SUB, LANES), jnp.float32)
         lane = lane_of(edge)
         for t in range(levels):
-            part = slice(t * SUB, (t + 1) * SUB)
-            edge = jnp.where(lane == 2 * t, carry[part], jnp.where(lane == 2 * t + 1, back[part], edge))
+            own = slice(t * SUB, (t + 1) * SUB)
+            edge = jnp.where(lane == 2 * t, carry[own], jnp.where(lane == 2 * t + 1, back[own], edge))
         edges[q, here, :] = edge
 
-    def find_state(q):
-        log = packed[0, q] * float(width)
+    def find_state(q, h):
+        here = part_rows(h)
+        log = packed[0, q, here, :] * float(width)
         eastward = lax.rem(lane_of(log), 2) == 0
-        total = edges[q] * jnp.exp(log * float(n_lon - 1))
+        total = edges[q, here, :] * jnp.exp(log * float(n_lon - 1))
         for step in range(1, n_lon):
             hops = jnp.where(eastward, float(step - 1), float(n_lon - step - 1))
-            total = total + edges_in[q, step - 1] * jnp.exp(log * hops)
+            total = total + edges_in[q, step - 1, here, :] * jnp.exp(log * hops)
         state[...] = total / (1.0 - jnp.exp(log * float(n_lon)))
 
-    def set_row(q, t, at, part):
-        rows[q, t, :, at] = part
-
-    def set_own(q, at, part):
-        gathered[q, pl.ds(pl.multiple_of(lat * depth, SUB), depth), at] = part
-
-    def correct(q, t, store):
+    def set_row(q, h, t, at, value):
+        rows[q, t, part_rows(h), at] = value
+
+    def set_own(q, h, at, value):
+        gathered[q, part_gathered(h), at] = value
+
+    def correct(q, h, t, store):
+        here = part_rows(h)
         incoming = state[...]
-        scale = spread_lane(packed[1, q], 2 * t)
-        stride, to_east, to_west = powers(spread_lane(packed[0, q], 2 * t))
+        scale = spread_lane(packed[1, q, here, :], 2 * t)
+        stride, to_east, to_west = powers(spread_lane(packed[0, q, here, :], 2 * t))
         carry = spread_lane(incoming, 2 * t) * scale
         back = spread_lane(incoming, 2 * t + 1) * scale
-        parts = []
+        pieces = []
         for c in range(chunks):
-            parts.append(scale * rows[q, t, :, c * LANES : (c + 1) * LANES] + to_east * carry)
+            pieces.append(scale * rows[q, t, here, c * LANES : (c + 1) * LANES] + to_east * carry)
             carry = carry * stride
         for c in range(chunks - 1, -1, -1):
-            parts[c] = parts[c] + to_west * back
+            pieces[c] = pieces[c] + to_west * back
             back = back * stride
         for c in range(chunks):
-            store(slice(c * LANES, (c + 1) * LANES), parts[c])
-
-    def first(q, _):
-        def scan(g, _):
+            store(slice(c * LANES, (c + 1) * LANES), pieces[c])
+
+    def first(unit, _):
+        q, h = unit // parts, lax.rem(unit, parts)
+
+        def scan(place, _):
+            g = h * (groups // parts) + place
+
             @pl.when(q == 0)
             def _():
                 field_copy(g).wait()
@@ -212,37 +225,37 @@
             scan_group(q, g)
             return 0
 
-        lax.fori_loop(0, groups, scan, 0)
-
-        @pl.when(q == 0)
+        lax.fori_loop(0, groups // parts, scan, 0)
+
+        @pl.when(unit == 0)
         def _():
             pl.semaphore_wait(barrier, n_lon - 1 + n_lat - 1)
 
         for step in range(1, n_lon):
-            edge_copy(q, step).start()
+            edge_copy(q, h, step).start()
         for step in range(1, n_lon):
-            edge_copy(q, step).wait()
-
-        find_state(q)
+            edge_copy(q, h, step).wait()
+        find_state(q, h)
 
         def ship(place, _):
             step = step_at(lat, place, n_lat)
             t = partner(lat, step, n_lat)
-            correct(q, t, functools.partial(set_row, q, t))
-            x_copy(q, step).start()
+            correct(q, h, t, functools.partial(set_row, q, h, t))
+            x_copy(q, h, step).start()
             return 0
 
         lax.fori_loop(0, n_lat - 1, ship, 0)
-        correct(q, lat, functools.partial(set_own, q))
+        correct(q, h, lat, functools.partial(set_own, q, h))
         return 0
 
-    lax.fori_loop(0, rounds, first, 0)
+    lax.fori_loop(0, rounds * parts, first, 0)
     weights_copy.wait()
     w_high[...], w_low[...] = split(weights[...])
 
     def second(q, _):
         for step in order:
-            x_copy(q, step).wait_recv()
+            for h in range(parts):
+                x_copy(q, h, step).wait_recv()
         tile = 256 if width % 256 == 0 else LANES
 
         def columns(n, _):
@@ -265,7 +278,8 @@
     def finish(q, _):
         own_copy(q).wait()
         for step in order:
-            x_copy(q, step).wait_send()
+            for h in range(parts):
+                x_copy(q, h, step).wait_send()
             y_copy(q, step).wait()
         return 0
 
@@ -276,6 +290,7 @@
     lev, depth, width = field.shape
     total = depth * n_lat
     rounds = lev // n_lat
+    parts = 3 if depth % (3 * SUB) == 0 else 1
     f32, bf16 = jnp.float32, jnp.bfloat16
     pair = jnp.stack([jnp.log1p(-rate), rate / (2.0 - rate)])
     pair = pair.reshape(2, n_lat, rounds, depth).transpose(0, 2, 3, 1)
@@ -301,13 +316,13 @@
             vmem((rounds, n_lat, depth, width), f32),
             vmem((rounds, depth, LANES), f32),
             vmem((rounds, n_lon - 1, depth, LANES), f32),
-            vmem((depth, LANES), f32),
+            vmem((depth // parts, LANES), f32),
             vmem((rounds, total, width), f32),
             vmem((rounds, total, width), f32),
-            dma((rounds, n_lon - 1)),
-            dma((rounds, n_lon - 1)),
-            dma((rounds, n_lat - 1)),
-            dma((rounds, n_lat - 1)),
+            dma((rounds, parts, n_lon - 1)),
+            dma((rounds, parts, n_lon - 1)),
+            dma((rounds, parts, n_lat - 1)),
+            dma((rounds, parts, n_lat - 1)),
             dma((rounds, n_lat - 1)),
             dma((rounds, n_lat - 1)),
             dma((rounds,)),

time: 441 us -> 432 us (0.980)
  Pallas kernels: 431 us -> 421 us
    pallas_call x1, Pallas kernels: 431 us -> 421 us  [on_device(): pl.pallas_call(functools.partial(kernel, n_lon, n_lat), out_shape=jax.Sha...]
where the time goes in v3:
time: 432 us; the launch traced here: 431 us
  Pallas kernels  421 us (97%)
  local copies, waits for them, and re-layouts  9.38 us (2%)
    pallas_call x1, Pallas kernels, on_device(): pl.pallas_call(functools.partial(kernel, n_lon, n_lat), out_shape=jax.Sha...  421 us

profile of v3, /device:TPU:9, one launch (start us, length us, event | category | flops | bytes accessed | tf_op | source)
XLA Modules:
  0.0 431.3 jit_solution(14263014332216577129)
XLA Ops:
  0.0 0.7 negate_log-plus-one_fusion
  0.8 0.2 copy.7
  1.0 0.8 pad.4.packed
  1.7 421.1 %shard_map.46 = f32[32,96,768]{2,1,0:T(8,128)} custom-call(f32[32,96,768]{2,1,0:T(8,128)} %field_hbm.1, f32[32,32]{1,0:T(8,128)} %vertical.1, f32[2,4,96,128]{3,2,1,0:T(8,128)} %pad.4.packed, f32[768,768]{1,0:T(8,128)} %weights_hbm.1), custom_call_target="tpu_custom_call" | custom-call | flops 11324620800 | bytes 18874368 | tf_op jit(solution)/shard_map/pallas_call | solution.py:299
  422.9 8.4 %copy.9 = f32[32,96,768]{2,1,0:T(8,128)} copy(f32[32,96,768]{2,1,0:T(8,128)} %shard_map.46) | data formatting | bytes 18874368
  (3 shorter events, 0.0 us)

commit v4 on v3

--- a/solution.py
+++ b/solution.py
@@ -286,6 +286,19 @@
     lax.fori_loop(0, rounds, finish, 0)
 
 
+def write_out(landed, out, sems):
+    count = sems.shape[0]
+    size = out.shape[0] // count
+    copies = [
+        pltpu.make_async_copy(landed.at[pl.ds(i * size, size)], out.at[pl.ds(i * size, size)], sems.at[i])
+        for i in range(count)
+    ]
+    for copy in copies:
+        copy.start()
+    for copy in copies:
+        copy.wait()
+
+
 def on_device(n_lon, n_lat, field, vertical, rate, lat_kernel):
     lev, depth, width = field.shape
     total = depth * n_lat
@@ -296,16 +309,16 @@
     pair = pair.reshape(2, n_lat, rounds, depth).transpose(0, 2, 3, 1)
     packed = jnp.pad(jnp.repeat(pair, 2, axis=3), ((0, 0), (0, 0), (0, 0), (0, LANES - 2 * n_lat)), constant_values=-1.0)
     vmem, dma = pltpu.VMEM, pltpu.SemaphoreType.DMA
-    return pl.pallas_call(
+    landed = pl.pallas_call(
         functools.partial(kernel, n_lon, n_lat),
-        out_shape=jax.ShapeDtypeStruct(field.shape, f32),
+        out_shape=pltpu.VMEM(field.shape, f32),
         in_specs=[
             pl.BlockSpec(memory_space=pl.ANY),
             pl.BlockSpec(memory_space=pltpu.VMEM),
             pl.BlockSpec(memory_space=pltpu.VMEM),
             pl.BlockSpec(memory_space=pl.ANY),
         ],
-        out_specs=pl.BlockSpec(memory_space=pl.ANY),
+        out_specs=pl.BlockSpec(memory_space=pltpu.VMEM),
         scratch_shapes=[
             vmem(field.shape, f32),
             vmem((total, total), f32),
@@ -330,12 +343,21 @@
             dma(()),
         ],
         compiler_params=pltpu.CompilerParams(
-            collective_id=0, has_side_effects=True, vmem_limit_bytes=60 * 1024 * 1024
+            collective_id=0, has_side_effects=True, vmem_limit_bytes=50 * 1024 * 1024
         ),
         cost_estimate=pl.CostEstimate(
             flops=6 * lev * depth * width * (total + lev), bytes_accessed=8 * lev * depth * width, transcendentals=0
         ),
     )(field, vertical, packed, lat_kernel)
+    return pl.pallas_call(
+        write_out,
+        out_shape=jax.ShapeDtypeStruct(field.shape, f32),
+        in_specs=[pl.BlockSpec(memory_space=pltpu.VMEM)],
+        out_specs=pl.BlockSpec(memory_space=pl.ANY),
+        scratch_shapes=[dma((rounds,))],
+        compiler_params=pltpu.CompilerParams(vmem_limit_bytes=12 * 1024 * 1024),
+        cost_estimate=pl.CostEstimate(flops=0, bytes_accessed=8 * lev * depth * width, transcendentals=0),
+    )(landed)
 
 
 def solution(mesh):

time: 432 us -> 427 us (0.988)
  local copies, waits for them, and re-layouts: 9.38 us -> 0.97 us
    unnamed x1 -> x0, local copies, waits for them, and re-layouts: 8.41 us -> none
    pallas_call x1 -> x2, Pallas kernels: 421 us -> 425 us  [the longest x1 421 us: on_device(): pl.pallas_call(functools.partial(kernel, n_lon, n_lat), out_shape=pltpu.V...]
where the time goes in v4:
time: 427 us; the launch traced here: 426 us
  Pallas kernels  425 us (100%)
    pallas_call x1, Pallas kernels, on_device(): pl.pallas_call(functools.partial(kernel, n_lon, n_lat), out_shape=pltpu.V...  421 us

profile of v4, /device:TPU:9, one launch (start us, length us, event | category | flops | bytes accessed | tf_op | source)
XLA Modules:
  0.0 426.5 jit_solution(6135923021597364805)
XLA Ops:
  0.0 0.7 negate_log-plus-one_fusion
  0.8 0.2 copy.7
  1.0 0.8 pad.4.packed
  1.7 421.0 %shard_map.46.landed = f32[32,96,768]{2,1,0:T(8,128)S(1)} custom-call(f32[32,96,768]{2,1,0:T(8,128)} %field_hbm.1, f32[32,32]{1,0:T(8,128)} %vertical.1, f32[2,4,96,128]{3,2,1,0:T(8,128)} %pad.4.packed, f32[768,768]{1,0:T(8,128)} %weights_hbm.1), custom_call_target="tpu_custom_call" | custom-call | flops 11324620800 | bytes 18874368 | tf_op jit(solution)/shard_map/pallas_call | solution.py:312
  422.8 3.7 shard_map.47
  (3 shorter events, 0.0 us)
